TPU v7x, 32 devices: a whole 2x2x4 slice. The times are simulated.
32 devices in a mesh: sub: 8 (over z, y), grp: 4 (over x, core).
Axes of the slice: x: 2, y: 2, z: 4, core: 2. Of those that a mesh axis runs over, the one named last changes fastest.
Arguments:
- right_side: float32 [512, 8192], P('grp', 'sub'), may hold values from -6 to 6
- operator_block: bfloat16 [8192, 1024], P('sub'), may hold values from -0.1875 to 0.1875
- operator_diag: float32 [8192], P('sub'), may hold values from 2 to 4
- solve_block: bfloat16 [8192, 1024], P('sub'), may hold values from -0.1875 to 0.1875
- solve_diag: float32 [8192], P('sub'), may hold values from 0.5 to 1.5
- upper_rows: int32 [8, 128], P('sub'), may hold values from 0 to 1023, as said below
- lower_rows: int32 [8, 128], P('sub'), may hold values from 0 to 1023, as said below
- couple_up: bfloat16 [1024, 128], P('sub'), may hold values from -0.5 to 0.5
- couple_down: bfloat16 [1024, 128], P('sub'), may hold values from -0.5 to 0.5
- coarse_basis: bfloat16 [64, 8192], P(None, 'sub'), may hold values from -0.75 to 0.75
- coarse_inverse: bfloat16 [512, 512], P(('sub', 'grp')), may hold values from -0.046875 to 0.046875
Outputs:
- solution: float32 [512, 8192], P('grp', 'sub')
Inputs may be any that keep to these rules, and one draw needn't show every extreme that they name: `upper_rows`: local row numbers within a subdomain of 1024 unknowns; the 128 entries of one subdomain are distinct, and none of them appears in lower_rows of the same subdomain. `lower_rows`: local row numbers within a subdomain of 1024 unknowns; the 128 entries of one subdomain are distinct, and none of them appears in upper_rows of the same subdomain.
All inputs are finite; a program needn't handle non-finite values.
Results may differ from a plain program's by a relative error of at most 0.0042.
Values may be sent and summed in bfloat16 or wider, within the bound.
A program may use at most 64 MiB of HBM per device.

v0:
```python
import jax
import jax.numpy as jnp
from jax import lax
from jax.sharding import PartitionSpec as P

ITERS = 3


EPS = 1e-06


def extended(block, sides, width):
    for axis, dim in sides:
        count = lax.axis_size(axis)
        forward = [(i, i + 1) for i in range(count - 1)]
        forward.append((count - 1, 0))
        backward = [(target, source) for source, target in forward]
        low = lax.ppermute(
            lax.slice_in_dim(block, block.shape[dim] - width, None, axis=dim), axis, forward
        )
        high = lax.ppermute(lax.slice_in_dim(block, 0, width, axis=dim), axis, backward)
        block = jnp.concatenate([low, block, high], axis=dim)
    return block


def contract_last(left, right):
    return lax.dot_general(
        left, right, (((1,), (1,)), ((), ())), preferred_element_type=jnp.float32
    )


def apply_operator(
    vector, operator_block, operator_diag, upper_list, lower_list, couple_up, couple_down
):
    vector_b = vector.astype(jnp.bfloat16)
    product = contract_last(vector_b, operator_block)
    face_count = upper_list.shape[0]
    upper_face = jnp.take(vector_b, upper_list, axis=1)
    lower_face = jnp.take(vector_b, lower_list, axis=1)
    two_faces = jnp.concatenate([lower_face, upper_face], axis=1)
    padded = extended(two_faces, (("sub", 1),), face_count)
    from_below = padded[:, :face_count]
    from_above = padded[:, 3 * face_count :]
    into_upper = jnp.dot(from_above, couple_up, preferred_element_type=jnp.float32)
    into_lower = jnp.dot(from_below, couple_down, preferred_element_type=jnp.float32)
    result = operator_diag[None, :] * vector + product
    result = result.at[:, upper_list].add(into_upper)
    result = result.at[:, lower_list].add(into_lower)
    return result


def apply_solve(vector, solve_block, solve_diag, coarse_basis, coarse_inverse):
    vector_b = vector.astype(jnp.bfloat16)
    local_term = contract_last(vector_b, solve_block)
    partial_res = contract_last(coarse_basis, vector_b).astype(jnp.bfloat16)
    widened = lax.all_gather(partial_res, "grp", axis=1, tiled=True)
    solved_part = jnp.dot(
        coarse_inverse,
        lax.all_gather(widened, "sub", axis=0, tiled=True),
        preferred_element_type=jnp.float32,
    ).astype(jnp.bfloat16)
    solved = lax.all_to_all(solved_part, "grp", split_axis=1, concat_axis=0, tiled=True)
    coarse_term = lax.dot_general(
        solved, coarse_basis, (((0,), (0,)), ((), ())), preferred_element_type=jnp.float32
    )
    return solve_diag[None, :] * vector + local_term + coarse_term


def norm_of(vector):
    squares = jnp.sum(vector * vector, axis=1)
    return jnp.sqrt(lax.psum(squares, "sub") + EPS)


def least_squares(initial_norm, columns):
    extent = len(columns)
    rotations = []
    target = [initial_norm] + [jnp.zeros_like(initial_norm) for _ in range(extent)]
    triangle = []
    for j in range(extent):
        column = list(columns[j])
        for i in range(j):
            cosine, sine_value = rotations[i]
            leading = cosine * column[i] + sine_value * column[i + 1]
            column[i + 1] = -sine_value * column[i] + cosine * column[i + 1]
            column[i] = leading
        radius = jnp.sqrt(column[j] * column[j] + column[j + 1] * column[j + 1])
        cosine = column[j] / radius
        sine_value = column[j + 1] / radius
        column[j] = radius
        rotations.append((cosine, sine_value))
        target[j + 1] = -sine_value * target[j]
        target[j] = cosine * target[j]
        triangle.append(column[: j + 1])
    coeffs = [None] * extent
    for j in reversed(range(extent)):
        partial_sum = target[j]
        for k in range(j + 1, extent):
            partial_sum = partial_sum - triangle[k][j] * coeffs[k]
        coeffs[j] = partial_sum / triangle[j][j]
    return coeffs


def on_device(
    right_side,
    operator_block,
    operator_diag,
    solve_block,
    solve_diag,
    upper_rows,
    lower_rows,
    couple_up,
    couple_down,
    coarse_basis,
    coarse_inverse,
):
    upper_list = upper_rows.reshape(-1)
    lower_list = lower_rows.reshape(-1)

    def precond(vector):
        return apply_solve(vector, solve_block, solve_diag, coarse_basis, coarse_inverse)

    residual = precond(right_side)
    initial_norm = norm_of(residual)
    krylov = [residual / initial_norm[:, None]]
    columns = []
    for iteration in range(ITERS):
        candidate = precond(
            apply_operator(
                krylov[iteration],
                operator_block,
                operator_diag,
                upper_list,
                lower_list,
                couple_up,
                couple_down,
            )
        )
        heights = []
        for i in range(iteration + 1):
            height_i = lax.psum(jnp.sum(candidate * krylov[i], axis=1), "sub")
            heights.append(height_i)
            candidate = candidate - height_i[:, None] * krylov[i]
        height = norm_of(candidate)
        heights.append(height)
        krylov.append(candidate / height[:, None])
        columns.append(heights)
    coeffs = least_squares(initial_norm, columns)
    solution = coeffs[0][:, None] * krylov[0]
    for j in range(1, ITERS):
        solution = solution + coeffs[j][:, None] * krylov[j]
    return solution


def solution(mesh):
    return jax.shard_map(
        on_device,
        mesh=mesh,
        in_specs=(
            P("grp", "sub"),
            P("sub", None),
            P("sub"),
            P("sub", None),
            P("sub"),
            P("sub", None),
            P("sub", None),
            P("sub", None),
            P("sub", None),
            P(None, "sub"),
            P(("sub", "grp"), None),
        ),
        out_specs=P("grp", "sub"),
        check_vma=False,
    )
```

profile of v0, /device:TPU:0, one launch (start us, length us, event | category | flops | bytes accessed | tf_op | source)
XLA Modules:
  0.0 463.0 jit_solution(12258683345657579884)
XLA Ops:
  1.5 6.2 %all_gather.24 = bf16[64,512]{1,0:T(8,128)(2,1)S(1)} all-gather(bf16[64,128]{1,0:T(8,128)(2,1)S(1)} %convolution_convert_fusion.7), channel_id=1, replica_groups=mesh['sub'=8,'grp'=4] {'grp'}, dimensions={1}, use_global_device_ids=true | all-gather | bytes 81920 | tf_op jit(solution)/shard_map/all_gather | solution.py:56
  7.7 32.6 %all_gather.25 = bf16[512,512]{1,0:T(8,128)(2,1)S(1)} all-gather(bf16[64,512]{1,0:T(8,128)(2,1)S(1)} %all_gather.24), channel_id=1, replica_groups=mesh['sub'=8,'grp'=4] {'sub'}, dimensions={0}, use_global_device_ids=true | all-gather | bytes 589824 | tf_op jit(solution)/shard_map/all_gather | solution.py:59
  41.7 3.2 all-to-all-start
  53.7 21.2 %psum.70 = f32[128]{0:T(128)S(1)} all-reduce(f32[128]{0:T(128)S(1)} %get-tuple-element.18), channel_id=1, replica_groups=mesh['sub'=8,'grp'=4] {'sub'}, use_global_device_ids=true, to_apply=%region_1.0 | all-reduce | flops 128 | bytes 1024 | tf_op jit(solution)/shard_map/psum | solution.py:71
  77.0 4.7 %collective-permute-start = (bf16[128,128]{0,1:T(8,128)(2,1)S(1)}, bf16[128,128]{0,1:T(8,128)(2,1)S(1)}, u32[]{:S(2)}, u32[]{:S(2)}) collective-permute-start(bf16[128,128]{0,1:T(8,128)(2,1)S(1)} %select_bitcast_fusion.5), channel_id=1, source_target_pairs={{4,0},{8,4},{12,8},{16,12},{20,16},{24,20},{28,24},{0,28},{5,1},{9... | collective-permute-start | bytes 98312 | tf_op jit(solution)/shard_map/ppermute | solution.py:21
  91.2 5.3 %all_gather.26 = bf16[64,512]{1,0:T(8,128)(2,1)S(1)} all-gather(bf16[64,128]{1,0:T(8,128)(2,1)S(1)} %fusion.1), channel_id=1, replica_groups=mesh['sub'=8,'grp'=4] {'grp'}, dimensions={1}, use_global_device_ids=true | all-gather | bytes 81920 | tf_op jit(solution)/shard_map/all_gather | solution.py:56
  96.4 31.3 %all_gather.27 = bf16[512,512]{1,0:T(8,128)(2,1)S(1)} all-gather(bf16[64,512]{1,0:T(8,128)(2,1)S(1)} %all_gather.26), channel_id=1, replica_groups=mesh['sub'=8,'grp'=4] {'sub'}, dimensions={0}, use_global_device_ids=true | all-gather | bytes 589824 | tf_op jit(solution)/shard_map/all_gather | solution.py:59
  128.5 3.2 all-to-all-start.1
  137.0 19.2 %psum.71 = f32[128]{0:T(128)S(1)} all-reduce(f32[128]{0:T(128)S(1)} %get-tuple-element.20), channel_id=1, replica_groups=mesh['sub'=8,'grp'=4] {'sub'}, use_global_device_ids=true, to_apply=%region_5.7 | all-reduce | flops 128 | bytes 1024 | tf_op jit(solution)/shard_map/psum | solution.py:140
  156.4 17.1 %psum.72 = f32[128]{0:T(128)S(1)} all-reduce(f32[128]{0:T(128)S(1)} %multiply_reduce_fusion.7), channel_id=1, replica_groups=mesh['sub'=8,'grp'=4] {'sub'}, use_global_device_ids=true, to_apply=%region_7.9 | all-reduce | flops 128 | bytes 1024 | tf_op jit(solution)/shard_map/psum | solution.py:71
  202.1 5.3 %all_gather.28 = bf16[64,512]{1,0:T(8,128)(2,1)S(1)} all-gather(bf16[64,128]{1,0:T(8,128)(2,1)S(1)} %fusion.3), channel_id=1, replica_groups=mesh['sub'=8,'grp'=4] {'grp'}, dimensions={1}, use_global_device_ids=true | all-gather | bytes 81920 | tf_op jit(solution)/shard_map/all_gather | solution.py:56
  207.3 31.5 %all_gather.29 = bf16[512,512]{1,0:T(8,128)(2,1)S(1)} all-gather(bf16[64,512]{1,0:T(8,128)(2,1)S(1)} %all_gather.28), channel_id=1, replica_groups=mesh['sub'=8,'grp'=4] {'sub'}, dimensions={0}, use_global_device_ids=true | all-gather | bytes 589824 | tf_op jit(solution)/shard_map/all_gather | solution.py:59
  248.8 18.0 %psum.73 = f32[128]{0:T(128)S(1)} all-reduce(f32[128]{0:T(128)S(1)} %get-tuple-element.22), channel_id=1, replica_groups=mesh['sub'=8,'grp'=4] {'sub'}, use_global_device_ids=true, to_apply=%region_11.13 | all-reduce | flops 128 | bytes 1024 | tf_op jit(solution)/shard_map/psum | solution.py:140
  268.1 18.3 %psum.74 = f32[128]{0:T(128)S(1)} all-reduce(f32[128]{0:T(128)S(1)} %multiply_reduce_fusion.5), channel_id=1, replica_groups=mesh['sub'=8,'grp'=4] {'sub'}, use_global_device_ids=true, to_apply=%region_13.15 | all-reduce | flops 128 | bytes 1024 | tf_op jit(solution)/shard_map/psum | solution.py:140
  288.4 18.2 %psum.75 = f32[128]{0:T(128)S(1)} all-reduce(f32[128]{0:T(128)S(1)} %get-tuple-element.14), channel_id=1, replica_groups=mesh['sub'=8,'grp'=4] {'sub'}, use_global_device_ids=true, to_apply=%region_15.17 | all-reduce | flops 128 | bytes 1024 | tf_op jit(solution)/shard_map/psum | solution.py:71
  313.0 3.5 convolution_add_fusion.5
  317.9 3.6 collective-permute-start.4
  334.5 5.3 %all_gather.30 = bf16[64,512]{1,0:T(8,128)(2,1)S(1)} all-gather(bf16[64,128]{1,0:T(8,128)(2,1)S(1)} %fusion.5), channel_id=1, replica_groups=mesh['sub'=8,'grp'=4] {'grp'}, dimensions={1}, use_global_device_ids=true | all-gather | bytes 81920 | tf_op jit(solution)/shard_map/all_gather | solution.py:56
  339.7 31.5 %all_gather.31 = bf16[512,512]{1,0:T(8,128)(2,1)S(1)} all-gather(bf16[64,512]{1,0:T(8,128)(2,1)S(1)} %all_gather.30), channel_id=1, replica_groups=mesh['sub'=8,'grp'=4] {'sub'}, dimensions={0}, use_global_device_ids=true | all-gather | bytes 589824 | tf_op jit(solution)/shard_map/all_gather | solution.py:59
  372.0 3.2 all-to-all-start.3
  381.1 21.2 %psum.76 = f32[128]{0:T(128)S(1)} all-reduce(f32[128]{0:T(128)S(1)} %get-tuple-element.24), channel_id=1, replica_groups=mesh['sub'=8,'grp'=4] {'sub'}, use_global_device_ids=true, to_apply=%region_19.21 | all-reduce | flops 128 | bytes 1024 | tf_op jit(solution)/shard_map/psum | solution.py:140
  403.7 17.1 %psum.77 = f32[128]{0:T(128)S(1)} all-reduce(f32[128]{0:T(128)S(1)} %multiply_reduce_fusion.2), channel_id=1, replica_groups=mesh['sub'=8,'grp'=4] {'sub'}, use_global_device_ids=true, to_apply=%region_21.23 | all-reduce | flops 128 | bytes 1024 | tf_op jit(solution)/shard_map/psum | solution.py:140
  423.1 19.1 %psum.78 = f32[128]{0:T(128)S(1)} all-reduce(f32[128]{0:T(128)S(1)} %get-tuple-element.12), channel_id=1, replica_groups=mesh['sub'=8,'grp'=4] {'sub'}, use_global_device_ids=true, to_apply=%region_23.25 | all-reduce | flops 128 | bytes 1024 | tf_op jit(solution)/shard_map/psum | solution.py:140
  443.6 17.2 %psum.79 = f32[128]{0:T(128)S(1)} all-reduce(f32[128]{0:T(128)S(1)} %multiply_reduce_fusion), channel_id=1, replica_groups=mesh['sub'=8,'grp'=4] {'sub'}, use_global_device_ids=true, to_apply=%region_25.27 | all-reduce | flops 128 | bytes 1024 | tf_op jit(solution)/shard_map/psum | solution.py:71
  (181 shorter events, 105.4 us)
Async XLA Ops:
  0.0 50.0 %copy-start = (bf16[1024,1024]{1,0:T(8,128)(2,1)S(1)}, bf16[1024,1024]{1,0:T(8,128)(2,1)}, u32[]{:S(2)}) copy-start(bf16[1024,1024]{1,0:T(8,128)(2,1)} %param.16) | copy-start | bytes 6291460
  0.0 50.0 %copy-start.2 = (f32[128,1024]{1,0:T(8,128)S(1)}, f32[128,1024]{1,0:T(8,128)}, u32[]{:S(2)}) copy-start(f32[128,1024]{1,0:T(8,128)} %param.13) | copy-start | bytes 1572868
  7.7 44.7 %copy-start.1 = (bf16[64,1024]{1,0:T(8,128)(2,1)S(1)}, bf16[64,1024]{1,0:T(8,128)(2,1)}, u32[]{:S(2)}) copy-start(bf16[64,1024]{1,0:T(8,128)(2,1)} %param.22) | copy-start | bytes 393220
  41.7 10.6 %all-to-all-start = ((bf16[16,4,128]{2,0,1:T(8,128)(2,1)}), bf16[16,4,128]{2,0,1:T(8,128)(2,1)S(1)}, u32[]{:S(2)}, u32[]{:S(2)}) async-start(bf16[16,4,128]{2,0,1:T(8,128)(2,1)} %bitcast.121), calls=%async_computation | async-start | bytes 32768 | tf_op jit(solution)/shard_map/all_to_all | solution.py:62
  76.8 9.4 %collective-permute-start.1 = (bf16[128,128]{0,1:T(8,128)(2,1)S(1)}, bf16[128,128]{0,1:T(8,128)(2,1)S(1)}, u32[]{:S(2)}, u32[]{:S(2)}) collective-permute-start(bf16[128,128]{0,1:T(8,128)(2,1)S(1)} %select_bitcast_fusion.4), channel_id=1, source_target_pairs={{0,4},{4,8},{8,12},{12,16},{16,20},{20,24},{24,28},{28,0},{1,5},{5... | collective-permute-start | bytes 98312 | tf_op jit(solution)/shard_map/ppermute | solution.py:18
  77.0 9.5 %collective-permute-start = (bf16[128,128]{0,1:T(8,128)(2,1)S(1)}, bf16[128,128]{0,1:T(8,128)(2,1)S(1)}, u32[]{:S(2)}, u32[]{:S(2)}) collective-permute-start(bf16[128,128]{0,1:T(8,128)(2,1)S(1)} %select_bitcast_fusion.5), channel_id=1, source_target_pairs={{4,0},{8,4},{12,8},{16,12},{20,16},{24,20},{28,24},{0,28},{5,1},{9... | collective-permute-start | bytes 98312 | tf_op jit(solution)/shard_map/ppermute | solution.py:21
  86.8 40.9 %copy-start.10 = (bf16[16,512]{1,0:T(8,128)(2,1)S(1)}, bf16[16,512]{1,0:T(8,128)(2,1)}, u32[]{:S(2)}) copy-start(bf16[16,512]{1,0:T(8,128)(2,1)} %param.23) | copy-start | bytes 49156
  88.4 43.4 %copy-start.13 = (f32[1024]{0:T(1024)S(1)}, f32[1024]{0:T(1024)}, u32[]{:S(2)}) copy-start(f32[1024]{0:T(1024)} %param.17) | copy-start | bytes 12292
  128.5 7.1 %all-to-all-start.1 = ((bf16[16,4,128]{2,0,1:T(8,128)(2,1)}), bf16[16,4,128]{2,0,1:T(8,128)(2,1)S(1)}, u32[]{:S(2)}, u32[]{:S(2)}) async-start(bf16[16,4,128]{2,0,1:T(8,128)(2,1)} %bitcast.120), calls=%async_computation.1 | async-start | bytes 32768 | tf_op jit(solution)/shard_map/all_to_all | solution.py:62
  137.0 36.6 %copy-start.3 = (f32[128,1024]{1,0:T(8,128)}, f32[128,1024]{1,0:T(8,128)S(1)}, u32[]{:S(2)}) copy-start(f32[128,1024]{1,0:T(8,128)S(1)} %get-tuple-element.21) | copy-start | bytes 1572868
  181.2 10.0 %collective-permute-start.3 = (bf16[128,128]{0,1:T(8,128)(2,1)S(1)}, bf16[128,128]{0,1:T(8,128)(2,1)S(1)}, u32[]{:S(2)}, u32[]{:S(2)}) collective-permute-start(bf16[128,128]{0,1:T(8,128)(2,1)S(1)} %select_bitcast_fusion.2), channel_id=1, source_target_pairs={{0,4},{4,8},{8,12},{12,16},{16,20},{20,24},{24,28},{28,0},{1,5},{5... | collective-permute-start | bytes 98312 | tf_op jit(solution)/shard_map/ppermute | solution.py:18
  183.3 8.3 %collective-permute-start.2 = (bf16[128,128]{0,1:T(8,128)(2,1)S(1)}, bf16[128,128]{0,1:T(8,128)(2,1)}, u32[]{:S(2)}, u32[]{:S(2)}) collective-permute-start(bf16[128,128]{0,1:T(8,128)(2,1)S(1)} %select_bitcast_fusion.3), channel_id=1, source_target_pairs={{4,0},{8,4},{12,8},{16,12},{20,16},{24,20},{28,24},{0,28},{5,1},{9... | collective-permute-start | bytes 98312 | tf_op jit(solution)/shard_map/ppermute | solution.py:21
  195.7 47.2 %copy-start.14 = (f32[1024]{0:T(1024)S(1)}, f32[1024]{0:T(1024)}, u32[]{:S(2)}) copy-start(f32[1024]{0:T(1024)} %param.17) | copy-start | bytes 12292
  239.7 7.1 %all-to-all-start.2 = ((bf16[16,4,128]{2,0,1:T(8,128)(2,1)}), bf16[16,4,128]{2,0,1:T(8,128)(2,1)S(1)}, u32[]{:S(2)}, u32[]{:S(2)}) async-start(bf16[16,4,128]{2,0,1:T(8,128)(2,1)} %bitcast.119), calls=%async_computation.2 | async-start | bytes 32768 | tf_op jit(solution)/shard_map/all_to_all | solution.py:62
  266.8 39.8 %copy-start.26 = (f32[128]{0:T(128)}, f32[128]{0:T(128)S(1)}, u32[]{:S(2)}) copy-start(f32[128]{0:T(128)S(1)} %psum.73) | copy-start | bytes 1540
  316.6 7.0 %collective-permute-start.5 = (bf16[128,128]{0,1:T(8,128)(2,1)S(1)}, bf16[128,128]{0,1:T(8,128)(2,1)S(1)}, u32[]{:S(2)}, u32[]{:S(2)}) collective-permute-start(bf16[128,128]{0,1:T(8,128)(2,1)S(1)} %select_bitcast_fusion), channel_id=1, source_target_pairs={{0,4},{4,8},{8,12},{12,16},{16,20},{20,24},{24,28},{28,0},{1,5},{5... | collective-permute-start | bytes 98312 | tf_op jit(solution)/shard_map/ppermute | solution.py:18
  317.9 6.0 %collective-permute-start.4 = (bf16[128,128]{0,1:T(8,128)(2,1)S(1)}, bf16[128,128]{0,1:T(8,128)(2,1)}, u32[]{:S(2)}, u32[]{:S(2)}) collective-permute-start(bf16[128,128]{0,1:T(8,128)(2,1)S(1)} %select_bitcast_fusion.1), channel_id=1, source_target_pairs={{4,0},{8,4},{12,8},{16,12},{20,16},{24,20},{28,24},{0,28},{5,1},{9... | collective-permute-start | bytes 98312 | tf_op jit(solution)/shard_map/ppermute | solution.py:21
  328.1 47.1 %copy-start.15 = (f32[1024]{0:T(1024)S(1)}, f32[1024]{0:T(1024)}, u32[]{:S(2)}) copy-start(f32[1024]{0:T(1024)} %param.17) | copy-start | bytes 12292
  372.0 7.1 %all-to-all-start.3 = ((bf16[16,4,128]{2,0,1:T(8,128)(2,1)}), bf16[16,4,128]{2,0,1:T(8,128)(2,1)S(1)}, u32[]{:S(2)}, u32[]{:S(2)}) async-start(bf16[16,4,128]{2,0,1:T(8,128)(2,1)} %bitcast.118), calls=%async_computation.3 | async-start | bytes 32768 | tf_op jit(solution)/shard_map/all_to_all | solution.py:62
  378.0 42.8 %copy-start.23 = (f32[128]{0:T(128)S(1)}, f32[128]{0:T(128)}, u32[]{:S(2)}) copy-start(f32[128]{0:T(128)} %copy-done.22) | copy-start | bytes 1540
  403.6 57.2 %copy-start.27 = (f32[128]{0:T(128)S(1)}, f32[128]{0:T(128)}, u32[]{:S(2)}) copy-start(f32[128]{0:T(128)} %copy-done.26) | copy-start | bytes 1540
  403.7 57.2 %copy-start.34 = (f32[128]{0:T(128)S(1)}, f32[128]{0:T(128)}, u32[]{:S(2)}) copy-start(f32[128]{0:T(128)} %copy-done.33) | copy-start | bytes 1540
  403.7 57.2 %copy-start.38 = (f32[128]{0:T(128)S(1)}, f32[128]{0:T(128)}, u32[]{:S(2)}) copy-start(f32[128]{0:T(128)} %copy-done.37) | copy-start | bytes 1540
  403.7 57.2 %copy-start.40 = (f32[128]{0:T(128)S(1)}, f32[128]{0:T(128)}, u32[]{:S(2)}) copy-start(f32[128]{0:T(128)} %copy-done.39) | copy-start | bytes 1540
  (27 other events, 327.7 us)
where the time goes:
time: 465 us; the launch traced here: 463 us
  blocking collectives  335 us (72%)
  other arithmetic  37.1 us (8%)
  matrix products  35.6 us (8%)
  starting transfers between devices  27.4 us (6%)
  local copies, waits for them, and re-layouts  23.7 us (5%)
    all_gather x4, blocking collectives, apply_solve(): lax.all_gather(widened, 'sub', axis=0, tiled=True)  127 us
    psum x6, blocking collectives, on_device(): height_i = lax.psum(jnp.sum(candidate * krylov[i], axis=1), 'sub')  113 us
    psum x4, blocking collectives, norm_of(): return jnp.sqrt(lax.psum(squares, 'sub') + EPS)  73.7 us
    dot_general x11, matrix products, contract_last(): lax.dot_general(left, right, (((1,), (1,)), ((), ())), preferred_element_...  24.7 us
    all_gather x4, blocking collectives, apply_solve(): widened = lax.all_gather(partial_res, 'grp', axis=1, tiled=True)  21.9 us
    all_to_all x4, starting transfers between devices, apply_solve(): lax.all_to_all(solved_part, 'grp', split_axis=1, concat_axis=0, tiled=True)  13 us
    ppermute x3, starting transfers between devices, extended(): lax.ppermute(lax.slice_in_dim(block, 0, width, axis=dim), axis, backward)  11.1 us
  transfers between devices with their start and end apart: 10, of which 3 were waited for; matrix products, arithmetic and copies ran while one was open for 6% of the time, Pallas kernels for 0%

commit v1 on v0

v1 whole, which is shorter than its diff:
```python
import functools

import jax
import jax.numpy as jnp
from jax import lax
from jax.experimental import pallas as pl
from jax.experimental.pallas import tpu as pltpu
from jax.sharding import PartitionSpec as P

ITERS = 3
EPS = 1e-06
TILE = 256
MESH = pl.DeviceIdType.MESH
BF = jnp.bfloat16
F32 = jnp.float32


def dot(a, b):
    return jnp.dot(a, b, preferred_element_type=F32)


def least_squares(initial_norm, columns):
    extent = len(columns)
    rotations = []
    target = [initial_norm] + [jnp.zeros_like(initial_norm) for _ in range(extent)]
    triangle = []
    for j in range(extent):
        column = list(columns[j])
        for i in range(j):
            cosine, sine_value = rotations[i]
            leading = cosine * column[i] + sine_value * column[i + 1]
            column[i + 1] = -sine_value * column[i] + cosine * column[i + 1]
            column[i] = leading
        radius = jnp.sqrt(column[j] * column[j] + column[j + 1] * column[j + 1])
        cosine = column[j] / radius
        sine_value = column[j + 1] / radius
        column[j] = radius
        rotations.append((cosine, sine_value))
        target[j + 1] = -sine_value * target[j]
        target[j] = cosine * target[j]
        triangle.append(column[: j + 1])
    coeffs = [None] * extent
    for j in reversed(range(extent)):
        partial_sum = target[j]
        for k in range(j + 1, extent):
            partial_sum = partial_sum - triangle[k][j] * coeffs[k]
        coeffs[j] = partial_sum / triangle[j][j]
    return coeffs


def each_peer(count, body):
    if count <= 8:
        for k in range(1, count):
            body(k)
    else:
        def step(k, carry):
            body(k)
            return carry
        lax.fori_loop(1, count, step, 0)


def kernel(
    n, g, rhs_h, op_h, od_h, sv_h, sd_h, up_h, lo_h, cu_h, cd_h, cb_h, ci_h, out_h,
    rhs_v, op_v, od_v, sv_v, sd_v, up_v, lo_v, cu_v, cd_v, cb_v, ci_v,
    odt, sdt, pg, ct, cbt, w, wb, vs, al, u, ub, loc, out_v,
    yall, fout, fin, vf, dall,
    in_sem, out_sem, ci_sem, ysem, fsem, dsem,
):
    me = lax.axis_index("sub")
    mg = lax.axis_index("grp")
    nloc = op_v.shape[0]
    kc = cb_v.shape[0]
    face = up_v.shape[1]
    part = ci_h.shape[0]
    tiles = nloc // TILE

    def rows(t):
        return pl.ds(t * TILE, TILE)

    loads = [
        pltpu.make_async_copy(src, dst, in_sem.at[i])
        for i, (src, dst) in enumerate([
            (rhs_h, rhs_v), (cb_h, cb_v), (sv_h, sv_v), (op_h, op_v), (od_h, od_v), (sd_h, sd_v),
            (up_h, up_v), (lo_h, lo_v), (cu_h, cu_v), (cd_h, cd_v),
            (ci_h, ci_v.at[pl.ds(pl.multiple_of(mg * part, part), part)]),
        ])
    ]
    for load in loads:
        load.start()

    barrier = pltpu.get_barrier_semaphore()
    each_peer(n, lambda k: pl.semaphore_signal(
        barrier, inc=1, device_id={"sub": lax.rem(me + k, n)}, device_id_type=MESH))
    each_peer(g, lambda k: pl.semaphore_signal(
        barrier, inc=1, device_id={"grp": lax.rem(mg + k, g)}, device_id_type=MESH))

    loads[0].wait()
    for t in range(tiles):
        tile = rhs_v[:, rows(t)].T
        u[rows(t), :] = tile
        ub[rows(t), :] = tile.astype(BF)
    loads[1].wait()
    loads[10].wait()

    pl.semaphore_wait(barrier, n - 1 + g - 1)

    my_part = pl.ds(pl.multiple_of(mg * part, part), part)

    def send_part(k):
        pltpu.make_async_remote_copy(
            ci_v.at[my_part], ci_v.at[my_part], ci_sem.at[0], ci_sem.at[1],
            device_id={"grp": lax.rem(mg + k, g)}, device_id_type=MESH).start()

    def y_start(p):
        slot = pl.ds(pl.multiple_of(me * kc, kc), kc)
        yall[p, slot, :] = dot(cb_v[...], ub[...]).astype(BF)

        def send(k):
            pltpu.make_async_remote_copy(
                yall.at[p, slot], yall.at[p, slot], ysem.at[p, 0], ysem.at[p, 1],
                device_id={"sub": lax.rem(me + k, n)}, device_id_type=MESH).start()
        each_peer(n, send)

    def y_wait(p, which):
        span = yall.at[p, pl.ds(0, (n - 1) * kc)]
        pltpu.make_async_copy(span, span, ysem.at[p, which]).wait()

    def d_wait(p, which):
        span = dall.at[p, pl.ds(0, (n - 1) * 8)]
        pltpu.make_async_copy(span, span, dsem.at[p, which]).wait()

    def ci_wait(which):
        span = ci_v.at[pl.ds(0, (g - 1) * part)]
        pltpu.make_async_copy(span, span, ci_sem.at[which]).wait()

    def face_copies(p):
        down = {"sub": lax.rem(me + n - 1, n)}
        up = {"sub": lax.rem(me + 1, n)}
        lower = pltpu.make_async_remote_copy(
            fout.at[p, pl.ds(face, face)], fin.at[p, pl.ds(0, face)],
            fsem.at[p, 0], fsem.at[p, 1], device_id=down, device_id_type=MESH)
        upper = pltpu.make_async_remote_copy(
            fout.at[p, pl.ds(0, face)], fin.at[p, pl.ds(face, face)],
            fsem.at[p, 2], fsem.at[p, 3], device_id=up, device_id_type=MESH)
        return lower, upper

    y_start(0)
    each_peer(g, send_part)

    for load in loads[4:10]:
        load.wait()
    for t in range(tiles):
        cols = rows(t)
        sdt[cols, :] = jnp.broadcast_to(sd_v[:, cols], (128, TILE)).T
        odt[cols, :] = jnp.broadcast_to(od_v[:, cols], (128, TILE)).T
        cbt[cols, :] = cb_v[:, cols].astype(F32).T.astype(BF)
        position = lax.broadcasted_iota(jnp.int32, (TILE, face), 0) + t * TILE
        for f, (list_v, couple_v) in enumerate(((up_v, cu_v), (lo_v, cd_v))):
            hot = (position == jnp.broadcast_to(list_v[...], (TILE, face))).astype(F32)
            pg[pl.ds(f * face, face), cols] = hot.T.astype(BF)
            ct[cols, pl.ds(f * face, face)] = lax.dot_general(
                hot.astype(BF), couple_v[...], (((1,), (1,)), ((), ())),
                preferred_element_type=F32).astype(BF)
    loads[2].wait()

    heights = []
    gram = {}
    initial_norm = None
    for j in range(-1, ITERS):
        p = j + 1
        for t in range(tiles):
            loc[rows(t), :] = sdt[rows(t), :] * u[rows(t), :] + dot(sv_v[rows(t), :], ub[...])
        if p == 0 and g > 1:
            ci_wait(1)
        y_wait(p, 1)
        c = dot(ci_v[...], yall[p]).astype(BF)
        sums = [None] * (2 * p + 1)
        for t in range(tiles):
            tile = loc[rows(t), :] + dot(cbt[rows(t), :], c)
            w[rows(t), :] = tile
            if j < ITERS - 1:
                high = tile.astype(BF)
                wb[rows(t), 0:128] = high
                wb[rows(t), 128:256] = (tile - high.astype(F32)).astype(BF)
            pairs = [(tile, tile)]
            basis = [vs[i, rows(t), :] for i in range(p)]
            pairs += [(tile, b) for b in basis]
            pairs += [(basis[p - 1], b) for b in basis]
            for i, (a, b) in enumerate(pairs):
                one = jnp.sum((a * b).reshape(TILE // 8, 8, 128), axis=0)
                sums[i] = one if sums[i] is None else sums[i] + one
        packed = [jnp.sum(s, axis=0, keepdims=True) for s in sums]
        packed += [jnp.zeros((8 - len(packed), 128), F32)]
        slot = pl.ds(pl.multiple_of(me * 8, 8), 8)
        dall[p, slot, :] = jnp.concatenate(packed, axis=0)

        def send_dots(k):
            pltpu.make_async_remote_copy(
                dall.at[p, slot], dall.at[p, slot], dsem.at[p, 0], dsem.at[p, 1],
                device_id={"sub": lax.rem(me + k, n)}, device_id_type=MESH).start()
        each_peer(n, send_dots)

        if j < ITERS - 1:
            fout[p] = dot(pg[...], wb[:, 0:128]).astype(BF)
            for copy in face_copies(p):
                copy.start()
            if p == 0:
                loads[3].wait()
            for t in range(tiles):
                both = dot(op_v[rows(t), :], wb[...])
                al[p, rows(t), :] = odt[rows(t), :] * w[rows(t), :] + (both[:, :128] + both[:, 128:])

        d_wait(p, 1)
        total = jnp.sum(dall[p].reshape(n, 8, 128), axis=0)
        square = total[0:1, :]
        h = [total[1 + i:2 + i, :] for i in range(p)]
        for i in range(p):
            gram[i, p - 1] = gram[p - 1, i] = total[1 + p + i:2 + p + i, :]
        for i in range(p):
            square = square - 2.0 * h[i] * h[i]
            for k in range(p):
                square = square + h[i] * h[k] * gram[i, k]
        norm = jnp.sqrt(jnp.maximum(square, 0.0) + EPS)
        if p == 0:
            initial_norm = norm
        else:
            heights.append(h + [norm])
        if j == ITERS - 1:
            break
        scale = 1.0 / norm

        def orthogonal(value, earlier):
            for i in range(p):
                value = value - h[i] * earlier(i)
            return value * scale

        for t in range(tiles):
            vs[p, rows(t), :] = orthogonal(w[rows(t), :], lambda i: vs[i, rows(t), :])
            al[p, rows(t), :] = orthogonal(al[p, rows(t), :], lambda i: al[i, rows(t), :])
        for copy in face_copies(p):
            copy.wait_recv()
        faces = orthogonal(fin[p].astype(F32), lambda i: vf[i])
        vf[p] = faces
        faces_b = faces.astype(BF)
        for t in range(tiles):
            tile = al[p, rows(t), :] + dot(ct[rows(t), :], faces_b)
            u[rows(t), :] = tile
            ub[rows(t), :] = tile.astype(BF)
        y_start(p + 1)

    coeffs = least_squares(initial_norm, heights)
    stores = []
    for t in range(tiles):
        tile = coeffs[0] * vs[0, rows(t), :]
        for i in range(1, ITERS):
            tile = tile + coeffs[i] * vs[i, rows(t), :]
        out_v[:, rows(t)] = tile.T
        store = pltpu.make_async_copy(out_v.at[:, rows(t)], out_h.at[:, rows(t)], out_sem.at[t])
        store.start()
        stores.append(store)
    if g > 1:
        ci_wait(0)
    for p in range(ITERS + 1):
        y_wait(p, 0)
        d_wait(p, 0)
        if p < ITERS:
            for copy in face_copies(p):
                copy.wait_send()
    for store in stores:
        store.wait()


def on_device(n, g, rhs, op, od, sv, sd, up, lo, cu, cd, cb, ci):
    nrhs, nloc = rhs.shape
    kc = cb.shape[0]
    face = up.shape[1]
    phases = ITERS + 1
    vmem = pltpu.VMEM
    dma = pltpu.SemaphoreType.DMA
    od, sd = od.reshape(1, nloc), sd.reshape(1, nloc)
    return pl.pallas_call(
        functools.partial(kernel, n, g),
        out_shape=jax.ShapeDtypeStruct(rhs.shape, F32),
        in_specs=[pl.BlockSpec(memory_space=pl.ANY)] * 11,
        out_specs=pl.BlockSpec(memory_space=pl.ANY),
        scratch_shapes=[
            vmem((nrhs, nloc), F32), vmem((nloc, nloc), BF), vmem((1, nloc), F32),
            vmem((nloc, nloc), BF), vmem((1, nloc), F32),
            vmem((1, face), jnp.int32), vmem((1, face), jnp.int32),
            vmem((face, face), BF), vmem((face, face), BF),
            vmem((kc, nloc), BF), vmem((kc, n * kc), BF),
            vmem((nloc, nrhs), F32), vmem((nloc, nrhs), F32),
            vmem((2 * face, nloc), BF), vmem((nloc, 2 * face), BF), vmem((nloc, kc), BF),
            vmem((nloc, nrhs), F32), vmem((nloc, 2 * nrhs), BF),
            vmem((ITERS, nloc, nrhs), F32), vmem((ITERS, nloc, nrhs), F32),
            vmem((nloc, nrhs), F32), vmem((nloc, nrhs), BF), vmem((nloc, nrhs), F32),
            vmem((nrhs, nloc), F32),
            vmem((phases, n * kc, nrhs), BF),
            vmem((ITERS, 2 * face, nrhs), BF), vmem((ITERS, 2 * face, nrhs), BF),
            vmem((ITERS, 2 * face, nrhs), F32), vmem((phases, n * 8, nrhs), F32),
            dma((11,)), dma((nloc // TILE,)), dma((2,)), dma((phases, 2)),
            dma((ITERS, 4)), dma((phases, 2)),
        ],
        compiler_params=pltpu.CompilerParams(
            collective_id=0, has_side_effects=True, vmem_limit_bytes=40 * 1024 * 1024),
    )(rhs, op, od, sv, sd, up, lo, cu, cd, cb, ci)


def solution(mesh):
    return jax.shard_map(
        functools.partial(on_device, mesh.shape["sub"], mesh.shape["grp"]),
        mesh=mesh,
        in_specs=(
            P("grp", "sub"),
            P("sub", None),
            P("sub"),
            P("sub", None),
            P("sub"),
            P("sub", None),
            P("sub", None),
            P("sub", None),
            P("sub", None),
            P(None, "sub"),
            P(("sub", "grp"), None),
        ),
        out_specs=P("grp", "sub"),
        check_vma=False,
    )
```

time: 465 us -> 61.2 us (0.13)
  blocking collectives: 335 us -> 0 us
  Pallas kernels: 0 us -> 49.9 us
  other arithmetic: 37.1 us -> 0 us
  matrix products: 35.6 us -> 0 us
  starting transfers between devices: 27.4 us -> 0 us
  local copies, waits for them, and re-layouts: 23.7 us -> 10.8 us
    psum x10 -> x0, blocking collectives: 187 us -> none  [the longest x6 113 us: on_device(): height_i = lax.psum(jnp.sum(candidate * krylov[i], axis=1), 'sub')]
    all_gather x8 -> x0, blocking collectives: 149 us -> none  [the longest x4 127 us: apply_solve(): lax.all_gather(widened, 'sub', axis=0, tiled=True)]
    pallas_call x0 -> x1, Pallas kernels: none -> 49.9 us  [on_device(): pl.pallas_call(functools.partial(kernel, n, g), out_shape=jax.ShapeDtypeS...]
    dot_general x25 -> x0, matrix products: 35.6 us -> none  [the longest x11 24.7 us: contract_last(): lax.dot_general(left, right, (((1,), (1,)), ((), ())), preferred_element_...]
    scatter-add x6 -> x0, other arithmetic: 15.6 us -> none  [the longest x3 7.81 us: apply_operator(): result = result.at[:, lower_list].add(into_lower)]
    ppermute x6 -> x0, starting transfers between devices: 14.4 us -> none  [the longest x3 11.1 us: extended(): lax.ppermute(lax.slice_in_dim(block, 0, width, axis=dim), axis, backward)]
    all_to_all x4 -> x0, starting transfers between devices: 13 us -> none  [apply_solve(): lax.all_to_all(solved_part, 'grp', split_axis=1, concat_axis=0, tiled=True)]
    unnamed x82 -> x23, local copies, waits for them, and re-layouts: 0.72 us -> 10.8 us
  transfers between devices with their start and end apart: 10 -> 0, of which waited for: 3 -> 0; matrix products, arithmetic and copies ran while one was open for 6% -> 0% of each run, Pallas kernels for 0% -> 0%
where the time goes in v1:
time: 61.2 us; the launch traced here: 60.7 us
  Pallas kernels  49.9 us (82%)
  local copies, waits for them, and re-layouts  10.8 us (18%)
    pallas_call x1, Pallas kernels, on_device(): pl.pallas_call(functools.partial(kernel, n, g), out_shape=jax.ShapeDtypeS...  49.9 us
    unnamed x23, local copies, waits for them, and re-layouts  10.8 us

profile of v1, /device:TPU:0, one launch (start us, length us, event | category | flops | bytes accessed | tf_op | source)
XLA Modules:
  0.0 60.7 jit_solution(17481533281090624811)
XLA Ops:
  0.0 0.0 copy-start
  0.0 1.6 %copy-done = bf16[1024,1024]{1,0:T(8,128)(2,1)S(1)} copy-done((bf16[1024,1024]{1,0:T(8,128)(2,1)S(1)}, bf16[1024,1024]{1,0:T(8,128)(2,1)}, u32[]{:S(2)}) %copy-start) | copy-done | bytes 2097176
  1.6 0.0 copy-start.1
  1.6 1.6 %copy-done.1 = bf16[1024,1024]{1,0:T(8,128)(2,1)S(1)} copy-done((bf16[1024,1024]{1,0:T(8,128)(2,1)S(1)}, bf16[1024,1024]{1,0:T(8,128)(2,1)}, u32[]{:S(2)}) %copy-start.1) | copy-done | bytes 2097176
  3.2 0.0 copy-start.2
  3.2 1.0 %copy-done.2 = f32[128,1024]{1,0:T(8,128)S(1)} copy-done((f32[128,1024]{1,0:T(8,128)S(1)}, f32[128,1024]{1,0:T(8,128)}, u32[]{:S(2)}) %copy-start.2) | copy-done | bytes 524312
  4.2 0.0 copy-start.3
  4.2 0.9 %copy-done.3 = bf16[64,1024]{1,0:T(8,128)(2,1)S(1)} copy-done((bf16[64,1024]{1,0:T(8,128)(2,1)S(1)}, bf16[64,1024]{1,0:T(8,128)(2,1)}, u32[]{:S(2)}) %copy-start.3) | copy-done | bytes 131096
  5.1 0.0 copy-start.4
  5.1 0.8 %copy-done.4 = bf16[128,128]{1,0:T(8,128)(2,1)S(1)} copy-done((bf16[128,128]{1,0:T(8,128)(2,1)S(1)}, bf16[128,128]{1,0:T(8,128)(2,1)}, u32[]{:S(2)}) %copy-start.4) | copy-done | bytes 32792
  5.9 0.0 copy-start.5
  5.9 0.8 %copy-done.5 = bf16[128,128]{1,0:T(8,128)(2,1)S(1)} copy-done((bf16[128,128]{1,0:T(8,128)(2,1)S(1)}, bf16[128,128]{1,0:T(8,128)(2,1)}, u32[]{:S(2)}) %copy-start.5) | copy-done | bytes 32792
  6.6 0.0 copy-start.6
  6.6 0.7 %copy-done.6 = bf16[16,512]{1,0:T(8,128)(2,1)S(1)} copy-done((bf16[16,512]{1,0:T(8,128)(2,1)S(1)}, bf16[16,512]{1,0:T(8,128)(2,1)}, u32[]{:S(2)}) %copy-start.6) | copy-done | bytes 16408
  7.4 0.0 copy-start.7
  7.4 0.7 %copy-done.7 = f32[1024]{0:T(1024)S(1)} copy-done((f32[1024]{0:T(1024)S(1)}, f32[1024]{0:T(1024)}, u32[]{:S(2)}) %copy-start.7) | copy-done | bytes 4120
  8.1 0.0 copy-start.8
  8.1 0.7 %copy-done.8 = f32[1024]{0:T(1024)S(1)} copy-done((f32[1024]{0:T(1024)S(1)}, f32[1024]{0:T(1024)}, u32[]{:S(2)}) %copy-start.8) | copy-done | bytes 4120
  8.7 0.0 copy-start.9
  8.7 0.7 %copy-done.9 = s32[1,128]{1,0:T(1,128)S(1)} copy-done((s32[1,128]{1,0:T(1,128)S(1)}, s32[1,128]{1,0:T(1,128)}, u32[]{:S(2)}) %copy-start.9) | copy-done | bytes 536
  9.4 0.0 copy-start.10
  9.4 0.7 %copy-done.10 = s32[1,128]{1,0:T(1,128)S(1)} copy-done((s32[1,128]{1,0:T(1,128)S(1)}, s32[1,128]{1,0:T(1,128)}, u32[]{:S(2)}) %copy-start.10) | copy-done | bytes 536
  10.1 49.9 %shard_map.109 = f32[128,1024]{1,0:T(8,128)S(1)} custom-call(f32[128,1024]{1,0:T(8,128)S(1)} %copy-done.2, bf16[1024,1024]{1,0:T(8,128)(2,1)S(1)} %copy-done, f32[1,1024]{1,0:T(1,128)S(1)} %bitcast.2, bf16[1024,1024]{1,0:T(8,128)(2,1)S(1)} %copy-done.1, f32[1,1024]{1,0:T(1,128)S(1)} %bitcast.3, s32[1,128]{1,0:T(1,128)S(1)} %copy-done.9, ...), custom_call_target="tpu_custom_call" | custom-call | tf_op jit(solution)/shard_map/pallas_call | solution.py:281
  59.9 0.8 %copy.13 = f32[128,1024]{1,0:T(8,128)} copy(f32[128,1024]{1,0:T(8,128)S(1)} %shard_map.109) | data formatting | bytes 1048576
Async XLA Ops:
  0.0 1.6 %copy-start = (bf16[1024,1024]{1,0:T(8,128)(2,1)S(1)}, bf16[1024,1024]{1,0:T(8,128)(2,1)}, u32[]{:S(2)}) copy-start(bf16[1024,1024]{1,0:T(8,128)(2,1)} %op_h.1) | copy-start | bytes 6291460
  1.6 1.6 %copy-start.1 = (bf16[1024,1024]{1,0:T(8,128)(2,1)S(1)}, bf16[1024,1024]{1,0:T(8,128)(2,1)}, u32[]{:S(2)}) copy-start(bf16[1024,1024]{1,0:T(8,128)(2,1)} %sv_h.1) | copy-start | bytes 6291460
  3.2 1.0 %copy-start.2 = (f32[128,1024]{1,0:T(8,128)S(1)}, f32[128,1024]{1,0:T(8,128)}, u32[]{:S(2)}) copy-start(f32[128,1024]{1,0:T(8,128)} %rhs_h.1) | copy-start | bytes 1572868
  4.2 0.9 %copy-start.3 = (bf16[64,1024]{1,0:T(8,128)(2,1)S(1)}, bf16[64,1024]{1,0:T(8,128)(2,1)}, u32[]{:S(2)}) copy-start(bf16[64,1024]{1,0:T(8,128)(2,1)} %cb_h.1) | copy-start | bytes 393220
  5.1 0.8 %copy-start.4 = (bf16[128,128]{1,0:T(8,128)(2,1)S(1)}, bf16[128,128]{1,0:T(8,128)(2,1)}, u32[]{:S(2)}) copy-start(bf16[128,128]{1,0:T(8,128)(2,1)} %cu_h.1) | copy-start | bytes 98308
  5.9 0.8 %copy-start.5 = (bf16[128,128]{1,0:T(8,128)(2,1)S(1)}, bf16[128,128]{1,0:T(8,128)(2,1)}, u32[]{:S(2)}) copy-start(bf16[128,128]{1,0:T(8,128)(2,1)} %cd_h.1) | copy-start | bytes 98308
  6.6 0.7 %copy-start.6 = (bf16[16,512]{1,0:T(8,128)(2,1)S(1)}, bf16[16,512]{1,0:T(8,128)(2,1)}, u32[]{:S(2)}) copy-start(bf16[16,512]{1,0:T(8,128)(2,1)} %ci_h.1) | copy-start | bytes 49156
  7.4 0.7 %copy-start.7 = (f32[1024]{0:T(1024)S(1)}, f32[1024]{0:T(1024)}, u32[]{:S(2)}) copy-start(f32[1024]{0:T(1024)} %param.13) | copy-start | bytes 12292
  8.1 0.7 %copy-start.8 = (f32[1024]{0:T(1024)S(1)}, f32[1024]{0:T(1024)}, u32[]{:S(2)}) copy-start(f32[1024]{0:T(1024)} %param.15) | copy-start | bytes 12292
  8.7 0.7 %copy-start.9 = (s32[1,128]{1,0:T(1,128)S(1)}, s32[1,128]{1,0:T(1,128)}, u32[]{:S(2)}) copy-start(s32[1,128]{1,0:T(1,128)} %up_h.1) | copy-start | bytes 1540
  9.4 0.7 %copy-start.10 = (s32[1,128]{1,0:T(1,128)S(1)}, s32[1,128]{1,0:T(1,128)}, u32[]{:S(2)}) copy-start(s32[1,128]{1,0:T(1,128)} %lo_h.1) | copy-start | bytes 1540

commit v2 on v1

--- a/solution.py
+++ b/solution.py
@@ -62,9 +62,9 @@
 def kernel(
     n, g, rhs_h, op_h, od_h, sv_h, sd_h, up_h, lo_h, cu_h, cd_h, cb_h, ci_h, out_h,
     rhs_v, op_v, od_v, sv_v, sd_v, up_v, lo_v, cu_v, cd_v, cb_v, ci_v,
-    odt, sdt, pg, ct, cbt, w, wb, vs, al, u, ub, loc, out_v,
-    yall, fout, fin, vf, dall,
-    in_sem, out_sem, ci_sem, ysem, fsem, dsem,
+    odt, sdt, pg, ct, cbt, w, wb, vs, zs, u, ub, loc, out_v,
+    yall, fout, fin, vf, dall, ub2, et, qout, qin, stage, gcol, cout, cin, cs,
+    in_sem, out_sem, ci_sem, ysem, fsem, dsem, qsem, gsem, csem,
 ):
     me = lax.axis_index("sub")
     mg = lax.axis_index("grp")
@@ -151,8 +151,6 @@
         load.wait()
     for t in range(tiles):
         cols = rows(t)
-        sdt[cols, :] = jnp.broadcast_to(sd_v[:, cols], (128, TILE)).T
-        odt[cols, :] = jnp.broadcast_to(od_v[:, cols], (128, TILE)).T
         cbt[cols, :] = cb_v[:, cols].astype(F32).T.astype(BF)
         position = lax.broadcasted_iota(jnp.int32, (TILE, face), 0) + t * TILE
         for f, (list_v, couple_v) in enumerate(((up_v, cu_v), (lo_v, cd_v))):
@@ -161,24 +159,73 @@
             ct[cols, pl.ds(f * face, face)] = lax.dot_general(
                 hot.astype(BF), couple_v[...], (((1,), (1,)), ((), ())),
                 preferred_element_type=F32).astype(BF)
+    qboth = dot(cb_v[...], ct[...]).astype(BF)
+    qout[pl.ds(0, kc), :] = qboth[:, face:]
+    qout[pl.ds(kc, kc), :] = qboth[:, :face]
+    q_copies = (
+        pltpu.make_async_remote_copy(
+            qout.at[pl.ds(0, kc)], qin.at[pl.ds(0, kc)], qsem.at[0], qsem.at[1],
+            device_id={"sub": lax.rem(me + n - 1, n)}, device_id_type=MESH),
+        pltpu.make_async_remote_copy(
+            qout.at[pl.ds(kc, kc)], qin.at[pl.ds(kc, kc)], qsem.at[2], qsem.at[3],
+            device_id={"sub": lax.rem(me + 1, n)}, device_id_type=MESH),
+    )
+    for copy in q_copies:
+        copy.start()
+    for t in range(tiles):
+        cols = rows(t)
+        sdt[cols, :] = jnp.broadcast_to(sd_v[:, cols], (128, TILE)).T
     loads[2].wait()
+    for t in range(tiles):
+        loc[rows(t), :] = sdt[rows(t), :] * u[rows(t), :] + dot(sv_v[rows(t), :], ub[...])
+
+    if g > 1:
+        ci_wait(1)
+    my_rows = pl.ds(pl.multiple_of(me * kc, kc), kc)
+    for s in range(n):
+        for i in range(3):
+            block = (s + i - 1 + n) % n
+            stage[s, :, pl.ds(i * kc, kc)] = ci_v[:, pl.ds(block * kc, kc)]
+        stage[s, :, pl.ds(3 * kc, kc)] = jnp.zeros((kc, kc), BF)
+
+    def send_columns(k):
+        to = lax.rem(me + k, n)
+        pltpu.make_async_remote_copy(
+            stage.at[to], gcol.at[my_rows], gsem.at[0], gsem.at[1],
+            device_id={"sub": to}, device_id_type=MESH).start()
+    each_peer(n, send_columns)
+    gcol[my_rows, :] = stage[me]
+
+    def g_wait(which):
+        span = gcol.at[pl.ds(0, (n - 1) * kc)]
+        pltpu.make_async_copy(span, span, gsem.at[which]).wait()
+
+    def c_wait(p, which):
+        span = cin.at[p, pl.ds(0, (n - 1) * kc)]
+        pltpu.make_async_copy(span, span, csem.at[p, which]).wait()
+
+    for t in range(tiles):
+        cols = rows(t)
+        odt[cols, :] = jnp.broadcast_to(od_v[:, cols], (128, TILE)).T
+        diag = sdt[cols, :]
+        diag = jnp.concatenate([diag] * (2 * face // 128), axis=1)
+        et[cols, :] = (diag * ct[cols, :].astype(F32) + dot(sv_v[cols, :], ct[...])).astype(BF)
+
+    y_wait(0, 1)
+    c = dot(ci_v[...], yall[0]).astype(BF)
+    for t in range(tiles):
+        w[rows(t), :] = loc[rows(t), :] + dot(cbt[rows(t), :], c)
 
     heights = []
     gram = {}
     initial_norm = None
     for j in range(-1, ITERS):
         p = j + 1
-        for t in range(tiles):
-            loc[rows(t), :] = sdt[rows(t), :] * u[rows(t), :] + dot(sv_v[rows(t), :], ub[...])
-        if p == 0 and g > 1:
-            ci_wait(1)
-        y_wait(p, 1)
-        c = dot(ci_v[...], yall[p]).astype(BF)
+        last = j == ITERS - 1
         sums = [None] * (2 * p + 1)
         for t in range(tiles):
-            tile = loc[rows(t), :] + dot(cbt[rows(t), :], c)
-            w[rows(t), :] = tile
-            if j < ITERS - 1:
+            tile = w[rows(t), :]
+            if not last:
                 high = tile.astype(BF)
                 wb[rows(t), 0:128] = high
                 wb[rows(t), 128:256] = (tile - high.astype(F32)).astype(BF)
@@ -200,7 +247,7 @@
                 device_id={"sub": lax.rem(me + k, n)}, device_id_type=MESH).start()
         each_peer(n, send_dots)
 
-        if j < ITERS - 1:
+        if not last:
             fout[p] = dot(pg[...], wb[:, 0:128]).astype(BF)
             for copy in face_copies(p):
                 copy.start()
@@ -208,7 +255,33 @@
                 loads[3].wait()
             for t in range(tiles):
                 both = dot(op_v[rows(t), :], wb[...])
-                al[p, rows(t), :] = odt[rows(t), :] * w[rows(t), :] + (both[:, :128] + both[:, 128:])
+                tile = odt[rows(t), :] * w[rows(t), :] + (both[:, :128] + both[:, 128:])
+                u[rows(t), :] = tile
+                high = tile.astype(BF)
+                ub2[rows(t), 0:128] = high
+                ub2[rows(t), 128:256] = (tile - high.astype(F32)).astype(BF)
+            if p == 0:
+                for copy in q_copies:
+                    copy.wait_recv()
+                g_wait(1)
+            shares = jnp.concatenate([
+                dot(qin[pl.ds(kc, kc), :], fout[p, pl.ds(face, face), :]),
+                dot(cb_v[...], ub2[:, 0:128]),
+                dot(qin[pl.ds(0, kc), :], fout[p, pl.ds(0, face), :]),
+                jnp.zeros((kc, 128), F32)], axis=0).astype(BF)
+            cout[p] = dot(gcol[...], shares).astype(BF)
+
+            def send_share(k):
+                to = lax.rem(me + k, n)
+                theirs = pl.ds(pl.multiple_of(to * kc, kc), kc)
+                pltpu.make_async_remote_copy(
+                    cout.at[p, theirs], cin.at[p, my_rows], csem.at[p, 0], csem.at[p, 1],
+                    device_id={"sub": to}, device_id_type=MESH).start()
+            each_peer(n, send_share)
+            cin[p, my_rows, :] = cout[p, my_rows, :]
+            for t in range(tiles):
+                both = dot(sv_v[rows(t), :], ub2[...])
+                zs[p, rows(t), :] = sdt[rows(t), :] * u[rows(t), :] + (both[:, :128] + both[:, 128:])
 
         d_wait(p, 1)
         total = jnp.sum(dall[p].reshape(n, 8, 128), axis=0)
@@ -225,7 +298,7 @@
             initial_norm = norm
         else:
             heights.append(h + [norm])
-        if j == ITERS - 1:
+        if last:
             break
         scale = 1.0 / norm
 
@@ -236,17 +309,20 @@
 
         for t in range(tiles):
             vs[p, rows(t), :] = orthogonal(w[rows(t), :], lambda i: vs[i, rows(t), :])
-            al[p, rows(t), :] = orthogonal(al[p, rows(t), :], lambda i: al[i, rows(t), :])
+            zs[p, rows(t), :] = orthogonal(zs[p, rows(t), :], lambda i: zs[i, rows(t), :])
         for copy in face_copies(p):
             copy.wait_recv()
         faces = orthogonal(fin[p].astype(F32), lambda i: vf[i])
         vf[p] = faces
         faces_b = faces.astype(BF)
+        c_wait(p, 1)
+        coarse = jnp.sum(cin[p].astype(F32).reshape(n, kc, 128), axis=0)
+        coarse = orthogonal(coarse, lambda i: cs[i])
+        cs[p] = coarse
+        coarse_b = coarse.astype(BF)
         for t in range(tiles):
-            tile = al[p, rows(t), :] + dot(ct[rows(t), :], faces_b)
-            u[rows(t), :] = tile
-            ub[rows(t), :] = tile.astype(BF)
-        y_start(p + 1)
+            w[rows(t), :] = zs[p, rows(t), :] + (
+                dot(et[rows(t), :], faces_b) + dot(cbt[rows(t), :], coarse_b))
 
     coeffs = least_squares(initial_norm, heights)
     stores = []
@@ -260,10 +336,14 @@
         stores.append(store)
     if g > 1:
         ci_wait(0)
+    y_wait(0, 0)
+    g_wait(0)
+    for copy in q_copies:
+        copy.wait_send()
     for p in range(ITERS + 1):
-        y_wait(p, 0)
         d_wait(p, 0)
         if p < ITERS:
+            c_wait(p, 0)
             for copy in face_copies(p):
                 copy.wait_send()
     for store in stores:
@@ -281,8 +361,8 @@
     return pl.pallas_call(
         functools.partial(kernel, n, g),
         out_shape=jax.ShapeDtypeStruct(rhs.shape, F32),
-        in_specs=[pl.BlockSpec(memory_space=pl.ANY)] * 11,
-        out_specs=pl.BlockSpec(memory_space=pl.ANY),
+        in_specs=[pl.BlockSpec(memory_space=pltpu.HBM)] * 11,
+        out_specs=pl.BlockSpec(memory_space=pltpu.HBM),
         scratch_shapes=[
             vmem((nrhs, nloc), F32), vmem((nloc, nloc), BF), vmem((1, nloc), F32),
             vmem((nloc, nloc), BF), vmem((1, nloc), F32),
@@ -295,14 +375,19 @@
             vmem((ITERS, nloc, nrhs), F32), vmem((ITERS, nloc, nrhs), F32),
             vmem((nloc, nrhs), F32), vmem((nloc, nrhs), BF), vmem((nloc, nrhs), F32),
             vmem((nrhs, nloc), F32),
-            vmem((phases, n * kc, nrhs), BF),
+            vmem((1, n * kc, nrhs), BF),
             vmem((ITERS, 2 * face, nrhs), BF), vmem((ITERS, 2 * face, nrhs), BF),
             vmem((ITERS, 2 * face, nrhs), F32), vmem((phases, n * 8, nrhs), F32),
-            dma((11,)), dma((nloc // TILE,)), dma((2,)), dma((phases, 2)),
-            dma((ITERS, 4)), dma((phases, 2)),
+            vmem((nloc, 2 * nrhs), BF), vmem((nloc, 2 * face), BF),
+            vmem((2 * kc, face), BF), vmem((2 * kc, face), BF),
+            vmem((n, kc, 4 * kc), BF), vmem((n * kc, 4 * kc), BF),
+            vmem((ITERS, n * kc, nrhs), BF), vmem((ITERS, n * kc, nrhs), BF),
+            vmem((ITERS, kc, nrhs), F32),
+            dma((11,)), dma((nloc // TILE,)), dma((2,)), dma((1, 2)),
+            dma((ITERS, 4)), dma((phases, 2)), dma((4,)), dma((2,)), dma((ITERS, 2)),
         ],
         compiler_params=pltpu.CompilerParams(
-            collective_id=0, has_side_effects=True, vmem_limit_bytes=40 * 1024 * 1024),
+            collective_id=0, has_side_effects=True, vmem_limit_bytes=64 * 1024 * 1024 - 65536),
     )(rhs, op, od, sv, sd, up, lo, cu, cd, cb, ci)
 
 

time: 61.2 us -> 44.8 us (0.73)
  local copies, waits for them, and re-layouts: 10.8 us -> 1.89 us
  Pallas kernels: 49.9 us -> 42.7 us
    unnamed x23 -> x1, local copies, waits for them, and re-layouts: 10.8 us -> 1.89 us
    pallas_call x1, Pallas kernels: 49.9 us -> 42.7 us  [on_device(): pl.pallas_call(functools.partial(kernel, n, g), out_shape=jax.ShapeDtypeS...]
where the time goes in v2:
time: 44.8 us; the launch traced here: 44.6 us
  Pallas kernels  42.7 us (95%)
  local copies, waits for them, and re-layouts  1.89 us (4%)
    pallas_call x1, Pallas kernels, on_device(): pl.pallas_call(functools.partial(kernel, n, g), out_shape=jax.ShapeDtypeS...  42.7 us
    unnamed x1, local copies, waits for them, and re-layouts  1.89 us

profile of v2, /device:TPU:0, one launch (start us, length us, event | category | flops | bytes accessed | tf_op | source)
XLA Modules:
  0.0 44.6 jit_solution(1378656968880322411)
XLA Ops:
  0.0 42.7 %shard_map.109 = f32[128,1024]{1,0:T(8,128)} custom-call(f32[128,1024]{1,0:T(8,128)} %rhs_h.1, bf16[1024,1024]{1,0:T(8,128)(2,1)} %op_h.1, f32[1,1024]{1,0:T(1,128)} %bitcast.2, bf16[1024,1024]{1,0:T(8,128)(2,1)} %sv_h.1, f32[1,1024]{1,0:T(1,128)} %bitcast.3, s32[1,128]{1,0:T(1,128)} %up_h.1, s32[1,128]{1,0:T(1,128)} %lo_h.1, bf16[128,128]{1,0:T(8,128)(2,1)} %cu_h.1, ...), custom_call_target="tpu_custom_call" | custom-call | tf_op jit(solution)/shard_map/pallas_call | solution.py:361
  42.7 1.9 %copy.13 = f32[128,1024]{1,0:T(8,128)} copy(f32[128,1024]{1,0:T(8,128)} %shard_map.109) | data formatting | bytes 1048576
